TPU v7x, 32 devices: a whole 2x2x4 slice. The times are simulated.
32 devices in a mesh: sec: 2 (over core), gx: 4 (over y, x), gy: 4 (over z).
Axes of the slice: x: 2, y: 2, z: 4, core: 2. Of those that a mesh axis runs over, the one named last changes fastest.
Arguments:
- adjoint_state: float32 [2, 10, 512, 512], P('sec', None, 'gx', 'gy'), may hold values from -6 to 6
- forcing: float32 [2, 10, 512, 512], P('sec', None, 'gx', 'gy'), may hold values from -6 to 6
- viscosity: float32 [2, 512, 512], P('sec', 'gx', 'gy'), may hold values from 0.5 to 4
- reaction: float32 [2, 512, 512], P('sec', 'gx', 'gy'), may hold values from 0.1 to 1
- source_patch: int32 [2, 2048], P('sec', ('gx', 'gy')), may hold values from 0 to 63
- owner: int32 [2, 2048, 1], P('sec', ('gx', 'gy')), may hold values from 0 to 15; in each aligned block of 128 rows (0 to 127, 128 to 255, ..., all dimensions but the last counted through in order) at most 16 rows name the same one
- cavity_map: int32 [2, 16, 16, 16], P('sec', ('gx', 'gy')), may hold values from 0 to 63
Outputs:
- adjoint_field: float32 [2, 10, 512, 512], P('sec', None, 'gx', 'gy')
Inputs may be any that keep to these rules, and one draw needn't show every extreme that they name: The entries of one device name each owner at most 16 times, a bound that some block reaches.
All inputs are finite; a program needn't handle non-finite values.
Results may differ from a plain program's by a relative error of at most 0.00002.
Values sent between devices are 32-bit elements; how exact they have to be, the bound alone decides.
A program may use at most 64 MiB of HBM per device.

v0:
```python
import jax
import jax.numpy as jnp
from jax import lax
from jax.sharding import PartitionSpec as P

PATCH = 2
PW = 128
SWEEPS = 8


OMEGA = 0.8
KAPPA = 0.5


def extended(cells, sides, width):
    for axis, dim in sides:
        count = lax.axis_size(axis)
        ends = count - 1
        head = lax.slice_in_dim(cells, 0, width, axis=dim)
        tail = lax.slice_in_dim(cells, cells.shape[dim] - width, cells.shape[dim], axis=dim)
        cells = jnp.concatenate(
            [
                lax.ppermute(tail, axis, [(i, (i + 1) % count) for i in range(ends)]),
                cells,
                lax.ppermute(head, axis, [((i + 1) % count, i) for i in range(ends)]),
            ],
            axis=dim,
        )
    return cells


def from_partner(block, axis, stride):
    count = lax.axis_size(axis)
    route = []
    for low in range(count):
        high = low | 1 << stride
        if high != low and high < count:
            route += [(low, high), (high, low)]
    return lax.ppermute(block, axis, route)


def relax(padded, visc, invd, force):
    center = padded[:, :, 1:-1, 1:-1]
    beside = padded[:, :, 2:, 1:-1] + padded[:, :, :-2, 1:-1]
    beside = beside + padded[:, :, 1:-1, 2:] + padded[:, :, 1:-1, :-2]
    return (1.0 - OMEGA) * center + OMEGA * invd * (force + visc * beside)


def single_sweep(field, visc, invd, force):
    padded = extended(field, (("gx", 2), ("gy", 3)), 1)
    return relax(padded, visc, invd, force)


def couple(field, source_patch, owner, cavity_map):
    levels, rows, cols = (field.shape[1], field.shape[2], field.shape[3])
    band_count = rows // PATCH
    strip_count = cols // PW
    grid = field[0].reshape(levels, band_count, PATCH, strip_count, PW)
    groups = cavity_map.shape[2]
    slots_per = cavity_map.shape[3]
    sources = source_patch[0]
    dest = owner[0, :, 0]
    onehot = (dest[:, None] == jnp.arange(groups, dtype=jnp.int32)[None, :]).astype(jnp.int32)
    before = jnp.cumsum(onehot, axis=0) - onehot
    rank = jnp.sum(before * onehot, axis=1)
    slot = dest * slots_per + rank
    src_band = sources // strip_count
    src_strip = sources % strip_count
    own = grid[:, src_band, :, src_strip, :]
    outgoing = jnp.zeros((groups * slots_per, levels, PATCH, PW), jnp.float32).at[slot].set(own)
    outgoing = outgoing.reshape(groups, slots_per, levels, PATCH, PW)
    crossed = from_partner(outgoing, "sec", 0)
    incoming = lax.all_to_all(crossed, ("gx", "gy"), split_axis=0, concat_axis=0, tiled=True)
    targets = cavity_map[0, 0].reshape(-1)
    tgt_band = targets // strip_count
    tgt_strip = targets % strip_count
    arrived = incoming.reshape(groups * slots_per, levels, PATCH, PW)
    local = grid[:, tgt_band, :, tgt_strip, :]
    answer = (local * jnp.tanh(arrived)).reshape(groups, slots_per, levels, PATCH, PW)
    updated = grid.at[:, tgt_band, :, tgt_strip, :].add(KAPPA * arrived)
    replies = lax.all_to_all(answer, ("gx", "gy"), split_axis=0, concat_axis=0, tiled=True)
    home = from_partner(replies, "sec", 0)
    back = home.reshape(groups * slots_per, levels, PATCH, PW)[slot]
    updated = updated.at[:, src_band, :, src_strip, :].add(back)
    return updated.reshape(1, levels, rows, cols)


def body(adjoint_state, forcing, viscosity, reaction, source_patch, owner, cavity_map):
    invd = 1.0 / (4.0 * viscosity + reaction)
    field = adjoint_state
    half = SWEEPS // 2
    visc = viscosity[:, None]
    inv_wide = invd[:, None]
    for step in range(half):
        field = single_sweep(field, visc, inv_wide, forcing)
    field = couple(field, source_patch, owner, cavity_map)
    for step in range(half):
        field = single_sweep(field, visc, inv_wide, forcing)
    return field


def solution(mesh):
    return jax.shard_map(
        body,
        mesh=mesh,
        in_specs=(
            P("sec", None, "gx", "gy"),
            P("sec", None, "gx", "gy"),
            P("sec", "gx", "gy"),
            P("sec", "gx", "gy"),
            P("sec", ("gx", "gy")),
            P("sec", ("gx", "gy"), None),
            P("sec", ("gx", "gy"), None, None),
        ),
        out_specs=P("sec", None, "gx", "gy"),
        check_vma=False,
    )
```

profile of v0, /device:TPU:0, one launch (start us, length us, event | category | flops | bytes accessed | tf_op | source)
XLA Modules:
  0.0 373.6 jit_solution(3170997130778900848)
XLA Ops:
  2.1 5.6 %collective-permute-start.1 = (f32[1,10,1,128]{3,2,1,0:T(1,128)S(1)}, f32[1,10,1,128]{3,2,1,0:T(1,128)S(1)}, u32[]{:S(2)}, u32[]{:S(2)}) collective-permute-start(f32[1,10,1,128]{3,2,1,0:T(1,128)S(1)} %get-tuple-element.39), channel_id=1, source_target_pairs={{0,4},{4,8},{8,12},{1,5},{5,9},{9,13},{2,6},{6,10},{10,14},{3,7},{... | collective-permute-start | bytes 15368 | tf_op jit(solution)/shard_map/ppermute | solution.py:23
  11.1 4.0 %collective-permute-start.3 = (f32[1,10,130,1]{2,1,3,0:T(8,128)S(1)}, f32[1,10,130,1]{2,1,3,0:T(8,128)S(1)}, u32[]{:S(2)}, u32[]{:S(2)}) collective-permute-start(f32[1,10,130,1]{2,1,3,0:T(8,128)S(1)} %copy.27), channel_id=1, source_target_pairs={{0,1},{1,2},{2,3},{4,5},{5,6},{6,7},{8,9},{9,10},{10,11},{12,13},{... | collective-permute-start | bytes 15608 | tf_op jit(solution)/shard_map/ppermute | solution.py:23
  17.4 4.0 %collective-permute-done.2 = f32[1,10,130,1]{2,1,3,0:T(8,128)S(1)} collective-permute-done((f32[1,10,130,1]{2,1,3,0:T(8,128)S(1)}, f32[1,10,130,1]{2,1,3,0:T(8,128)S(1)}, u32[]{:S(2)}, u32[]{:S(2)}) %collective-permute-start.2) | collective-permute-done | bytes 5232 | tf_op jit(solution)/shard_map/ppermute | solution.py:25
  25.8 4.9 %collective-permute-start.5 = (f32[1,10,1,128]{3,2,1,0:T(1,128)S(1)}, f32[1,10,1,128]{3,2,1,0:T(1,128)S(1)}, u32[]{:S(2)}, u32[]{:S(2)}) collective-permute-start(f32[1,10,1,128]{3,2,1,0:T(1,128)S(1)} %get-tuple-element.37), channel_id=1, source_target_pairs={{0,4},{4,8},{8,12},{1,5},{5,9},{9,13},{2,6},{6,10},{10,14},{3,7},{... | collective-permute-start | bytes 15368 | tf_op jit(solution)/shard_map/ppermute | solution.py:23
  38.9 4.0 %collective-permute-done.6 = f32[1,10,130,1]{2,1,3,0:T(8,128)S(1)} collective-permute-done((f32[1,10,130,1]{2,1,3,0:T(8,128)S(1)}, f32[1,10,130,1]{2,1,3,0:T(8,128)S(1)}, u32[]{:S(2)}, u32[]{:S(2)}) %collective-permute-start.6) | collective-permute-done | bytes 5232 | tf_op jit(solution)/shard_map/ppermute | solution.py:25
  45.1 5.7 %collective-permute-start.9 = (f32[1,10,1,128]{3,2,1,0:T(1,128)S(1)}, f32[1,10,1,128]{3,2,1,0:T(1,128)S(1)}, u32[]{:S(2)}, u32[]{:S(2)}) collective-permute-start(f32[1,10,1,128]{3,2,1,0:T(1,128)S(1)} %get-tuple-element.35), channel_id=1, source_target_pairs={{0,4},{4,8},{8,12},{1,5},{5,9},{9,13},{2,6},{6,10},{10,14},{3,7},{... | collective-permute-start | bytes 15368 | tf_op jit(solution)/shard_map/ppermute | solution.py:23
  65.1 5.7 %collective-permute-start.13 = (f32[1,10,1,128]{3,2,1,0:T(1,128)S(1)}, f32[1,10,1,128]{3,2,1,0:T(1,128)S(1)}, u32[]{:S(2)}, u32[]{:S(2)}) collective-permute-start(f32[1,10,1,128]{3,2,1,0:T(1,128)S(1)} %get-tuple-element.33), channel_id=1, source_target_pairs={{0,4},{4,8},{8,12},{1,5},{5,9},{9,13},{2,6},{6,10},{10,14},{3,7},{... | collective-permute-start | bytes 15368 | tf_op jit(solution)/shard_map/ppermute | solution.py:23
  88.0 15.5 %scatter_fusion = f32[256,10,2,128]{3,2,1,0:T(2,128)} fusion(f32[256,10,2,128]{3,2,1,0:T(2,128)} %broadcast_in_dim.2, s32[128]{0:T(128)S(1)} %fusion.57, f32[128,10,2,128]{3,2,1,0:T(2,128)S(1)} %copy-done.2), kind=kCustom, calls=%fused_computation.3 | custom fusion | bytes 3932672 | tf_op jit(solution)/shard_map/scatter | solution.py:70
  103.5 5.2 %collective-permute-done.16 = f32[16,16,10,2,128]{4,3,2,1,0:T(2,128)} collective-permute-done((f32[16,16,10,2,128]{4,3,2,1,0:T(2,128)}, f32[16,16,10,2,128]{4,3,2,1,0:T(2,128)}, u32[]{:S(2)}, u32[]{:S(2)}) %collective-permute-start.16) | collective-permute-done | bytes 2621472 | tf_op jit(solution)/shard_map/ppermute | solution.py:39
  108.8 6.8 %all-to-all-start = ((f32[16,16,10,2,128]{4,3,2,1,0:T(2,128)}), f32[16,16,10,2,128]{4,3,2,1,0:T(2,128)}, u32[]{:S(2)}, u32[]{:S(2)}) async-start(f32[16,16,10,2,128]{4,3,2,1,0:T(2,128)} %collective-permute-done.16), calls=%async_computation | async-start | bytes 5242880 | tf_op jit(solution)/shard_map/all_to_all | solution.py:73
  115.7 5.8 %gather_fusion.1 = f32[256,10,2,128]{3,2,1,0:T(2,128)} fusion(f32[10,64,2,1,128]{4,2,3,1,0:T(2,128)S(1)} %bitcast.36, s32[256]{0:T(256)S(1)} %bitcast.41), kind=kCustom, calls=%fused_computation.1 | custom fusion | bytes 5244928 | tf_op jit(solution)/shard_map/gather | solution.py:78
  121.6 57.8 %all-to-all-done = f32[16,16,10,2,128]{4,3,2,1,0:T(2,128)} async-done(((f32[16,16,10,2,128]{4,3,2,1,0:T(2,128)}), f32[16,16,10,2,128]{4,3,2,1,0:T(2,128)}, u32[]{:S(2)}, u32[]{:S(2)}) %all-to-all-start) | async-done | bytes 2621472 | tf_op jit(solution)/shard_map/all_to_all | solution.py:73
  179.4 7.1 %tanh_multiply_fusion = (f32[16,16,10,2,128]{4,3,2,1,0:T(2,128)S(1)}, f32[16,16,10,2,128]{4,3,2,1,0:T(2,128)}) fusion(f32[16,16,10,2,128]{4,3,2,1,0:T(2,128)} %bitcast.43, f32[16,16,10,2,128]{4,3,2,1,0:T(2,128)} %all-to-all-done), kind=kLoop, calls=%fused_computation.6 | loop fusion | flops 1310720 | bytes 10485760 | tf_op jit(solution)/shard_map/mul | solution.py:79
  186.4 64.0 %all_to_all.10 = f32[16,16,10,2,128]{4,3,2,1,0:T(2,128)} all-to-all(f32[16,16,10,2,128]{4,3,2,1,0:T(2,128)S(1)} %get-tuple-element.7), channel_id=1, replica_groups=mesh['sec'=2,'gx'=4,'gy'=4] {'gx','gy'}, dimensions={0} | all-to-all | bytes 5242880 | tf_op jit(solution)/shard_map/all_to_all | solution.py:81
  250.4 31.0 %scatter_fusion.1 = f32[10,64,2,128]{3,2,1,0:T(2,128)S(1)} fusion(f32[10,64,2,128]{3,2,1,0:T(2,128)S(1)} %bitcast.37, s32[256]{0:T(256)S(1)} %bitcast.53, f32[256,10,2,128]{3,2,1,0:T(2,128)} %bitcast.42), kind=kCustom, calls=%fused_computation.4 | custom fusion | flops 655360 | bytes 7865344 | tf_op jit(solution)/shard_map/scatter-add | solution.py:80
  285.2 11.6 %scatter_fusion.2 = f32[10,64,2,128]{3,2,1,0:T(2,128)S(1)} fusion(f32[10,64,2,128]{3,2,1,0:T(2,128)S(1)} %scatter_fusion.1, s32[128]{0:T(128)S(1)} %get-tuple-element.41, f32[128,10,2,128]{3,2,1,0:T(2,128)S(1)} %gather_fusion.2), kind=kCustom, calls=%fused_computation.5 | custom fusion | flops 327680 | bytes 3932672 | tf_op jit(solution)/shard_map/scatter-add | solution.py:84
  298.2 4.5 %collective-permute-start.19 = (f32[1,10,1,128]{3,2,1,0:T(1,128)S(1)}, f32[1,10,1,128]{3,2,1,0:T(1,128)S(1)}, u32[]{:S(2)}, u32[]{:S(2)}) collective-permute-start(f32[1,10,1,128]{3,2,1,0:T(1,128)S(1)} %get-tuple-element.31), channel_id=1, source_target_pairs={{0,4},{4,8},{8,12},{1,5},{5,9},{9,13},{2,6},{6,10},{10,14},{3,7},{... | collective-permute-start | bytes 15368 | tf_op jit(solution)/shard_map/ppermute | solution.py:23
  308.5 4.0 %collective-permute-done.20 = f32[1,10,130,1]{2,1,3,0:T(8,128)S(1)} collective-permute-done((f32[1,10,130,1]{2,1,3,0:T(8,128)S(1)}, f32[1,10,130,1]{2,1,3,0:T(8,128)S(1)}, u32[]{:S(2)}, u32[]{:S(2)}) %collective-permute-start.20) | collective-permute-done | bytes 5232 | tf_op jit(solution)/shard_map/ppermute | solution.py:25
  314.8 4.8 %collective-permute-start.23 = (f32[1,10,1,128]{3,2,1,0:T(1,128)S(1)}, f32[1,10,1,128]{3,2,1,0:T(1,128)S(1)}, u32[]{:S(2)}, u32[]{:S(2)}) collective-permute-start(f32[1,10,1,128]{3,2,1,0:T(1,128)S(1)} %get-tuple-element.29), channel_id=1, source_target_pairs={{0,4},{4,8},{8,12},{1,5},{5,9},{9,13},{2,6},{6,10},{10,14},{3,7},{... | collective-permute-start | bytes 15368 | tf_op jit(solution)/shard_map/ppermute | solution.py:23
  326.4 4.0 %collective-permute-done.24 = f32[1,10,130,1]{2,1,3,0:T(8,128)S(1)} collective-permute-done((f32[1,10,130,1]{2,1,3,0:T(8,128)S(1)}, f32[1,10,130,1]{2,1,3,0:T(8,128)S(1)}, u32[]{:S(2)}, u32[]{:S(2)}) %collective-permute-start.24) | collective-permute-done | bytes 5232 | tf_op jit(solution)/shard_map/ppermute | solution.py:25
  334.6 5.7 %collective-permute-start.27 = (f32[1,10,1,128]{3,2,1,0:T(1,128)S(1)}, f32[1,10,1,128]{3,2,1,0:T(1,128)S(1)}, u32[]{:S(2)}, u32[]{:S(2)}) collective-permute-start(f32[1,10,1,128]{3,2,1,0:T(1,128)S(1)} %get-tuple-element.27), channel_id=1, source_target_pairs={{0,4},{4,8},{8,12},{1,5},{5,9},{9,13},{2,6},{6,10},{10,14},{3,7},{... | collective-permute-start | bytes 15368 | tf_op jit(solution)/shard_map/ppermute | solution.py:23
  347.5 4.0 %collective-permute-done.28 = f32[1,10,130,1]{2,1,3,0:T(8,128)S(1)} collective-permute-done((f32[1,10,130,1]{2,1,3,0:T(8,128)S(1)}, f32[1,10,130,1]{2,1,3,0:T(8,128)S(1)}, u32[]{:S(2)}, u32[]{:S(2)}) %collective-permute-start.28) | collective-permute-done | bytes 5232 | tf_op jit(solution)/shard_map/ppermute | solution.py:25
  355.7 5.7 %collective-permute-start.31 = (f32[1,10,1,128]{3,2,1,0:T(1,128)S(1)}, f32[1,10,1,128]{3,2,1,0:T(1,128)S(1)}, u32[]{:S(2)}, u32[]{:S(2)}) collective-permute-start(f32[1,10,1,128]{3,2,1,0:T(1,128)S(1)} %get-tuple-element.25), channel_id=1, source_target_pairs={{0,4},{4,8},{8,12},{1,5},{5,9},{9,13},{2,6},{6,10},{10,14},{3,7},{... | collective-permute-start | bytes 15368 | tf_op jit(solution)/shard_map/ppermute | solution.py:23
  367.8 4.0 %collective-permute-done.32 = f32[1,10,130,1]{2,1,3,0:T(8,128)S(1)} collective-permute-done((f32[1,10,130,1]{2,1,3,0:T(8,128)S(1)}, f32[1,10,130,1]{2,1,3,0:T(8,128)S(1)}, u32[]{:S(2)}, u32[]{:S(2)}) %collective-permute-start.32) | collective-permute-done | bytes 5232 | tf_op jit(solution)/shard_map/ppermute | solution.py:25
  (142 shorter events, 97.2 us)
Async XLA Ops:
  0.8 6.9 %collective-permute-start = (f32[1,10,1,128]{3,2,1,0:T(1,128)S(1)}, f32[1,10,1,128]{3,2,1,0:T(1,128)S(1)}, u32[]{:S(2)}, u32[]{:S(2)}) collective-permute-start(f32[1,10,1,128]{3,2,1,0:T(1,128)S(1)} %get-tuple-element.40), channel_id=1, source_target_pairs={{4,0},{8,4},{12,8},{5,1},{9,5},{13,9},{6,2},{10,6},{14,10},{7,3},{... | collective-permute-start | bytes 15368 | tf_op jit(solution)/shard_map/ppermute | solution.py:25
  2.1 6.9 %collective-permute-start.1 = (f32[1,10,1,128]{3,2,1,0:T(1,128)S(1)}, f32[1,10,1,128]{3,2,1,0:T(1,128)S(1)}, u32[]{:S(2)}, u32[]{:S(2)}) collective-permute-start(f32[1,10,1,128]{3,2,1,0:T(1,128)S(1)} %get-tuple-element.39), channel_id=1, source_target_pairs={{0,4},{4,8},{8,12},{1,5},{5,9},{9,13},{2,6},{6,10},{10,14},{3,7},{... | collective-permute-start | bytes 15368 | tf_op jit(solution)/shard_map/ppermute | solution.py:23
  11.1 6.0 %collective-permute-start.3 = (f32[1,10,130,1]{2,1,3,0:T(8,128)S(1)}, f32[1,10,130,1]{2,1,3,0:T(8,128)S(1)}, u32[]{:S(2)}, u32[]{:S(2)}) collective-permute-start(f32[1,10,130,1]{2,1,3,0:T(8,128)S(1)} %copy.27), channel_id=1, source_target_pairs={{0,1},{1,2},{2,3},{4,5},{5,6},{6,7},{8,9},{9,10},{10,11},{12,13},{... | collective-permute-start | bytes 15608 | tf_op jit(solution)/shard_map/ppermute | solution.py:23
  15.7 5.6 %collective-permute-start.2 = (f32[1,10,130,1]{2,1,3,0:T(8,128)S(1)}, f32[1,10,130,1]{2,1,3,0:T(8,128)S(1)}, u32[]{:S(2)}, u32[]{:S(2)}) collective-permute-start(f32[1,10,130,1]{2,1,3,0:T(8,128)S(1)} %copy.25), channel_id=1, source_target_pairs={{1,0},{2,1},{3,2},{5,4},{6,5},{7,6},{9,8},{10,9},{11,10},{13,12},{... | collective-permute-start | bytes 15608 | tf_op jit(solution)/shard_map/ppermute | solution.py:25
  24.5 6.2 %collective-permute-start.4 = (f32[1,10,1,128]{3,2,1,0:T(1,128)S(1)}, f32[1,10,1,128]{3,2,1,0:T(1,128)S(1)}, u32[]{:S(2)}, u32[]{:S(2)}) collective-permute-start(f32[1,10,1,128]{3,2,1,0:T(1,128)S(1)} %get-tuple-element.38), channel_id=1, source_target_pairs={{4,0},{8,4},{12,8},{5,1},{9,5},{13,9},{6,2},{10,6},{14,10},{7,3},{... | collective-permute-start | bytes 15368 | tf_op jit(solution)/shard_map/ppermute | solution.py:25
  25.8 6.3 %collective-permute-start.5 = (f32[1,10,1,128]{3,2,1,0:T(1,128)S(1)}, f32[1,10,1,128]{3,2,1,0:T(1,128)S(1)}, u32[]{:S(2)}, u32[]{:S(2)}) collective-permute-start(f32[1,10,1,128]{3,2,1,0:T(1,128)S(1)} %get-tuple-element.37), channel_id=1, source_target_pairs={{0,4},{4,8},{8,12},{1,5},{5,9},{9,13},{2,6},{6,10},{10,14},{3,7},{... | collective-permute-start | bytes 15368 | tf_op jit(solution)/shard_map/ppermute | solution.py:23
  37.1 5.8 %collective-permute-start.6 = (f32[1,10,130,1]{2,1,3,0:T(8,128)S(1)}, f32[1,10,130,1]{2,1,3,0:T(8,128)S(1)}, u32[]{:S(2)}, u32[]{:S(2)}) collective-permute-start(f32[1,10,130,1]{2,1,3,0:T(8,128)S(1)} %copy.29), channel_id=1, source_target_pairs={{1,0},{2,1},{3,2},{5,4},{6,5},{7,6},{9,8},{10,9},{11,10},{13,12},{... | collective-permute-start | bytes 15608 | tf_op jit(solution)/shard_map/ppermute | solution.py:25
  43.8 7.3 %collective-permute-start.8 = (f32[1,10,1,128]{3,2,1,0:T(1,128)S(1)}, f32[1,10,1,128]{3,2,1,0:T(1,128)S(1)}, u32[]{:S(2)}, u32[]{:S(2)}) collective-permute-start(f32[1,10,1,128]{3,2,1,0:T(1,128)S(1)} %get-tuple-element.36), channel_id=1, source_target_pairs={{4,0},{8,4},{12,8},{5,1},{9,5},{13,9},{6,2},{10,6},{14,10},{7,3},{... | collective-permute-start | bytes 15368 | tf_op jit(solution)/shard_map/ppermute | solution.py:25
  45.1 7.0 %collective-permute-start.9 = (f32[1,10,1,128]{3,2,1,0:T(1,128)S(1)}, f32[1,10,1,128]{3,2,1,0:T(1,128)S(1)}, u32[]{:S(2)}, u32[]{:S(2)}) collective-permute-start(f32[1,10,1,128]{3,2,1,0:T(1,128)S(1)} %get-tuple-element.35), channel_id=1, source_target_pairs={{0,4},{4,8},{8,12},{1,5},{5,9},{9,13},{2,6},{6,10},{10,14},{3,7},{... | collective-permute-start | bytes 15368 | tf_op jit(solution)/shard_map/ppermute | solution.py:23
  57.2 5.6 %collective-permute-start.10 = (f32[1,10,130,1]{2,1,3,0:T(8,128)S(1)}, f32[1,10,130,1]{2,1,3,0:T(8,128)S(1)}, u32[]{:S(2)}, u32[]{:S(2)}) collective-permute-start(f32[1,10,130,1]{2,1,3,0:T(8,128)S(1)} %copy.33), channel_id=1, source_target_pairs={{1,0},{2,1},{3,2},{5,4},{6,5},{7,6},{9,8},{10,9},{11,10},{13,12},{... | collective-permute-start | bytes 15608 | tf_op jit(solution)/shard_map/ppermute | solution.py:25
  63.8 7.0 %collective-permute-start.12 = (f32[1,10,1,128]{3,2,1,0:T(1,128)S(1)}, f32[1,10,1,128]{3,2,1,0:T(1,128)S(1)}, u32[]{:S(2)}, u32[]{:S(2)}) collective-permute-start(f32[1,10,1,128]{3,2,1,0:T(1,128)S(1)} %get-tuple-element.34), channel_id=1, source_target_pairs={{4,0},{8,4},{12,8},{5,1},{9,5},{13,9},{6,2},{10,6},{14,10},{7,3},{... | collective-permute-start | bytes 15368 | tf_op jit(solution)/shard_map/ppermute | solution.py:25
  65.1 7.0 %collective-permute-start.13 = (f32[1,10,1,128]{3,2,1,0:T(1,128)S(1)}, f32[1,10,1,128]{3,2,1,0:T(1,128)S(1)}, u32[]{:S(2)}, u32[]{:S(2)}) collective-permute-start(f32[1,10,1,128]{3,2,1,0:T(1,128)S(1)} %get-tuple-element.33), channel_id=1, source_target_pairs={{0,4},{4,8},{8,12},{1,5},{5,9},{9,13},{2,6},{6,10},{10,14},{3,7},{... | collective-permute-start | bytes 15368 | tf_op jit(solution)/shard_map/ppermute | solution.py:23
  75.6 5.6 %collective-permute-start.14 = (f32[1,10,130,1]{2,1,3,0:T(8,128)S(1)}, f32[1,10,130,1]{2,1,3,0:T(8,128)S(1)}, u32[]{:S(2)}, u32[]{:S(2)}) collective-permute-start(f32[1,10,130,1]{2,1,3,0:T(8,128)S(1)} %copy.37), channel_id=1, source_target_pairs={{1,0},{2,1},{3,2},{5,4},{6,5},{7,6},{9,8},{10,9},{11,10},{13,12},{... | collective-permute-start | bytes 15608 | tf_op jit(solution)/shard_map/ppermute | solution.py:25
  108.8 70.6 %all-to-all-start = ((f32[16,16,10,2,128]{4,3,2,1,0:T(2,128)}), f32[16,16,10,2,128]{4,3,2,1,0:T(2,128)}, u32[]{:S(2)}, u32[]{:S(2)}) async-start(f32[16,16,10,2,128]{4,3,2,1,0:T(2,128)} %collective-permute-done.16), calls=%async_computation | async-start | bytes 5242880 | tf_op jit(solution)/shard_map/all_to_all | solution.py:73
  250.4 31.0 %collective-permute-start.17 = (f32[16,16,10,2,128]{4,3,2,1,0:T(2,128)}, f32[16,16,10,2,128]{4,3,2,1,0:T(2,128)}, u32[]{:S(2)}, u32[]{:S(2)}) collective-permute-start(f32[16,16,10,2,128]{4,3,2,1,0:T(2,128)} %all_to_all.10), channel_id=1, source_target_pairs={{0,16},{16,0},{1,17},{17,1},{2,18},{18,2},{3,19},{19,3},{4,20},{20... | collective-permute-start | bytes 7864328 | tf_op jit(solution)/shard_map/ppermute | solution.py:39
  296.9 5.9 %collective-permute-start.18 = (f32[1,10,1,128]{3,2,1,0:T(1,128)S(1)}, f32[1,10,1,128]{3,2,1,0:T(1,128)S(1)}, u32[]{:S(2)}, u32[]{:S(2)}) collective-permute-start(f32[1,10,1,128]{3,2,1,0:T(1,128)S(1)} %get-tuple-element.32), channel_id=1, source_target_pairs={{4,0},{8,4},{12,8},{5,1},{9,5},{13,9},{6,2},{10,6},{14,10},{7,3},{... | collective-permute-start | bytes 15368 | tf_op jit(solution)/shard_map/ppermute | solution.py:25
  298.2 5.9 %collective-permute-start.19 = (f32[1,10,1,128]{3,2,1,0:T(1,128)S(1)}, f32[1,10,1,128]{3,2,1,0:T(1,128)S(1)}, u32[]{:S(2)}, u32[]{:S(2)}) collective-permute-start(f32[1,10,1,128]{3,2,1,0:T(1,128)S(1)} %get-tuple-element.31), channel_id=1, source_target_pairs={{0,4},{4,8},{8,12},{1,5},{5,9},{9,13},{2,6},{6,10},{10,14},{3,7},{... | collective-permute-start | bytes 15368 | tf_op jit(solution)/shard_map/ppermute | solution.py:23
  313.5 6.1 %collective-permute-start.22 = (f32[1,10,1,128]{3,2,1,0:T(1,128)S(1)}, f32[1,10,1,128]{3,2,1,0:T(1,128)S(1)}, u32[]{:S(2)}, u32[]{:S(2)}) collective-permute-start(f32[1,10,1,128]{3,2,1,0:T(1,128)S(1)} %get-tuple-element.30), channel_id=1, source_target_pairs={{4,0},{8,4},{12,8},{5,1},{9,5},{13,9},{6,2},{10,6},{14,10},{7,3},{... | collective-permute-start | bytes 15368 | tf_op jit(solution)/shard_map/ppermute | solution.py:25
  314.8 6.1 %collective-permute-start.23 = (f32[1,10,1,128]{3,2,1,0:T(1,128)S(1)}, f32[1,10,1,128]{3,2,1,0:T(1,128)S(1)}, u32[]{:S(2)}, u32[]{:S(2)}) collective-permute-start(f32[1,10,1,128]{3,2,1,0:T(1,128)S(1)} %get-tuple-element.29), channel_id=1, source_target_pairs={{0,4},{4,8},{8,12},{1,5},{5,9},{9,13},{2,6},{6,10},{10,14},{3,7},{... | collective-permute-start | bytes 15368 | tf_op jit(solution)/shard_map/ppermute | solution.py:23
  324.8 5.6 %collective-permute-start.24 = (f32[1,10,130,1]{2,1,3,0:T(8,128)S(1)}, f32[1,10,130,1]{2,1,3,0:T(8,128)S(1)}, u32[]{:S(2)}, u32[]{:S(2)}) collective-permute-start(f32[1,10,130,1]{2,1,3,0:T(8,128)S(1)} %copy.47), channel_id=1, source_target_pairs={{1,0},{2,1},{3,2},{5,4},{6,5},{7,6},{9,8},{10,9},{11,10},{13,12},{... | collective-permute-start | bytes 15608 | tf_op jit(solution)/shard_map/ppermute | solution.py:25
  333.3 7.0 %collective-permute-start.26 = (f32[1,10,1,128]{3,2,1,0:T(1,128)S(1)}, f32[1,10,1,128]{3,2,1,0:T(1,128)S(1)}, u32[]{:S(2)}, u32[]{:S(2)}) collective-permute-start(f32[1,10,1,128]{3,2,1,0:T(1,128)S(1)} %get-tuple-element.28), channel_id=1, source_target_pairs={{4,0},{8,4},{12,8},{5,1},{9,5},{13,9},{6,2},{10,6},{14,10},{7,3},{... | collective-permute-start | bytes 15368 | tf_op jit(solution)/shard_map/ppermute | solution.py:25
  334.6 7.0 %collective-permute-start.27 = (f32[1,10,1,128]{3,2,1,0:T(1,128)S(1)}, f32[1,10,1,128]{3,2,1,0:T(1,128)S(1)}, u32[]{:S(2)}, u32[]{:S(2)}) collective-permute-start(f32[1,10,1,128]{3,2,1,0:T(1,128)S(1)} %get-tuple-element.27), channel_id=1, source_target_pairs={{0,4},{4,8},{8,12},{1,5},{5,9},{9,13},{2,6},{6,10},{10,14},{3,7},{... | collective-permute-start | bytes 15368 | tf_op jit(solution)/shard_map/ppermute | solution.py:23
  354.4 7.0 %collective-permute-start.30 = (f32[1,10,1,128]{3,2,1,0:T(1,128)S(1)}, f32[1,10,1,128]{3,2,1,0:T(1,128)S(1)}, u32[]{:S(2)}, u32[]{:S(2)}) collective-permute-start(f32[1,10,1,128]{3,2,1,0:T(1,128)S(1)} %get-tuple-element.26), channel_id=1, source_target_pairs={{4,0},{8,4},{12,8},{5,1},{9,5},{13,9},{6,2},{10,6},{14,10},{7,3},{... | collective-permute-start | bytes 15368 | tf_op jit(solution)/shard_map/ppermute | solution.py:25
  355.7 7.0 %collective-permute-start.31 = (f32[1,10,1,128]{3,2,1,0:T(1,128)S(1)}, f32[1,10,1,128]{3,2,1,0:T(1,128)S(1)}, u32[]{:S(2)}, u32[]{:S(2)}) collective-permute-start(f32[1,10,1,128]{3,2,1,0:T(1,128)S(1)} %get-tuple-element.25), channel_id=1, source_target_pairs={{0,4},{4,8},{8,12},{1,5},{5,9},{9,13},{2,6},{6,10},{10,14},{3,7},{... | collective-permute-start | bytes 15368 | tf_op jit(solution)/shard_map/ppermute | solution.py:23
  (18 other events, 128.9 us)
where the time goes:
time: 378 us; the launch traced here: 374 us
  waiting for transfers between devices  105 us (28%)
  starting transfers between devices  91.7 us (24%)
  blocking collectives  64 us (17%)
  other arithmetic  62 us (16%)
  local copies, waits for them, and re-layouts  50.3 us (13%)
    all_to_all x1, blocking collectives, couple(): lax.all_to_all(answer, ('gx', 'gy'), split_axis=0, concat_axis=0, tiled=T...  64 us
    ppermute x16, starting transfers between devices, extended(): lax.ppermute(tail, axis, [(i, (i + 1) % count) for i in range(ends)])  63.8 us
    all_to_all x1, waiting for transfers between devices, couple(): lax.all_to_all(crossed, ('gx', 'gy'), split_axis=0, concat_axis=0, tiled=...  57.8 us
    ppermute x16, waiting for transfers between devices, extended(): lax.ppermute(head, axis, [((i + 1) % count, i) for i in range(ends)])  31.8 us
    scatter-add x1, other arithmetic, couple(): updated = grid.at[:, tgt_band, :, tgt_strip, :].add(KAPPA * arrived)  31 us
    ppermute x16, starting transfers between devices, extended(): lax.ppermute(head, axis, [((i + 1) % count, i) for i in range(ends)])  21 us
    scatter x1, local copies, waits for them, and re-layouts, couple(): jnp.zeros((groups * slots_per, levels, PATCH, PW), jnp.float32).at[slot]  15.5 us
    scatter-add x1, other arithmetic, couple(): updated = updated.at[:, src_band, :, src_strip, :].add(back)  11.6 us
  transfers between devices with their start and end apart: 35, of which 18 were waited for; matrix products, arithmetic and copies ran while one was open for 12% of the time, Pallas kernels for 0%

commit v1 on v0

v1 whole, which is shorter than its diff:
```python
import functools

import jax
import jax.numpy as jnp
from jax import lax
from jax.experimental import pallas as pl
from jax.experimental.pallas import tpu as pltpu
from jax.sharding import PartitionSpec as P

OMEGA = 0.8
KAPPA = 0.5
HALF = 4
EDGE = 8
LANES = 128
MESH = pl.DeviceIdType.MESH
BF16 = jnp.bfloat16
F32 = jnp.float32


def iota(shape, dim):
    return lax.broadcasted_iota(jnp.int32, shape, dim)


def kernel(
    n_gx, n_gy, groups, cap, levels, chunk,
    x_ref, f_ref, v_ref, r_ref, src_ref, own_ref, map_ref, out_ref,
    xe, fe, be, rs1, rr1, ps1, pr1, rs2, rr2, ps2, pr2,
    tz, tp, weights, pieces, gz, parts, arrived,
    halo_send, halo_recv, tz_send, tz_recv, tp_send, tp_recv,
    z_send, z_recv, p_send, p_recv,
):
    sec, gx, gy = lax.axis_index("sec"), lax.axis_index("gx"), lax.axis_index("gy")
    rows = x_ref.shape[2]
    tall = rows + 2 * EDGE
    chunks = levels // chunk
    has = {-1: gx > 0, 0: True, 1: gx < n_gx - 1}
    has_y = {-1: gy > 0, 0: True, 1: gy < n_gy - 1}
    around = [(a, b) for a in (-1, 0, 1) for b in (-1, 0, 1) if (a, b) != (0, 0)]

    def exists(a, b):
        if a == 0:
            return has_y[b]
        if b == 0:
            return has[a]
        return jnp.logical_and(has[a], has_y[b])

    lane = iota((LANES, LANES), 1)
    row = iota((LANES, LANES), 0)
    named = jnp.where(own_ref[0] == lane, 1.0, 0.0).astype(BF16)
    earlier = jnp.where(lane < row, 1.0, 0.0).astype(BF16)
    before = jnp.dot(earlier, named, preferred_element_type=F32)
    rank = jnp.sum(before * named.astype(F32), axis=1, keepdims=True)
    source = jnp.sum(
        jnp.where(lane == row, src_ref[...].astype(F32) + 1.0, 0.0), axis=1, keepdims=True
    )
    ranked = jnp.where(rank == lane.astype(F32), source, 0.0).astype(BF16)
    slots = lax.dot_general(
        named, ranked, (((0,), (0,)), ((), ())), preferred_element_type=F32
    )
    tz[gy, 0:groups] = slots[0:groups]
    tz[gy, groups : 2 * groups] = jnp.full((groups, LANES), -1.0, F32)
    tz[gy, groups : 2 * groups, 0:cap] = map_ref[0, 0].astype(F32)

    inv = OMEGA / (4.0 * v_ref[0] + r_ref[0])
    be[...] = jnp.zeros_like(be)
    be[EDGE : EDGE + rows, 0:LANES] = inv * v_ref[0]
    for l in range(levels):
        fe[l, EDGE : EDGE + rows, 0:LANES] = inv * f_ref[0, l]

    def pack(planes, rs, ps):
        small = iota((rows, LANES), 1)
        for first in range(0, len(planes), 16):
            packed = jnp.zeros((rows, LANES), F32)
            for k, read in enumerate(planes[first : first + 16]):
                tile = read()
                rs[0, first + k] = tile[0:EDGE]
                rs[1, first + k] = tile[rows - EDGE : rows]
                low = tile if k == 0 else pltpu.roll(tile, 8 * k, 1)
                high = tile if k == 15 else pltpu.roll(tile, 8 * k + 8, 1)
                packed = jnp.where(small // 4 == 2 * k, low, packed)
                packed = jnp.where(small // 4 == 2 * k + 1, high, packed)
            ps[first // 16] = packed

    def halo_copy(phase, a, b, rs, rr, ps, pr):
        if b == 0:
            src, dst = rs.at[(a + 1) // 2], rr.at[(1 - a) // 2]
        else:
            side = (1 - b) // 2
            if a == 0:
                src, dst = ps, pr.at[side, :, EDGE : EDGE + rows]
            elif a == 1:
                src, dst = ps.at[:, rows - EDGE : rows], pr.at[side, :, 0:EDGE]
            else:
                src, dst = ps.at[:, 0:EDGE], pr.at[side, :, EDGE + rows : tall]
        k = around.index((a, b))
        return pltpu.make_async_remote_copy(
            src_ref=src, dst_ref=dst,
            send_sem=halo_send.at[phase, k], recv_sem=halo_recv.at[phase, k],
            device_id=(sec, gx + a, gy + b), device_id_type=MESH,
        )

    def halo_start(phase, *refs):
        for a, b in around:
            @pl.when(exists(a, b))
            def _():
                halo_copy(phase, a, b, *refs).start()

    def halo_wait(phase, rs, rr, ps, pr):
        for a, b in around:
            @pl.when(exists(-a, -b))
            def _():
                halo_copy(phase, a, b, rs, rr, ps, pr).wait_recv()

            @pl.when(exists(a, b))
            def _():
                halo_copy(phase, a, b, rs, rr, ps, pr).wait_send()

    def beside(pr, k):
        small = iota((tall, LANES), 1)
        at = 8 * (k % 16)
        right, left = pr[1, k // 16], pr[0, k // 16]
        right = right if at == 0 else pltpu.roll(right, LANES - at, 1)
        left = left if at == 120 else pltpu.roll(left, 120 - at, 1)
        return jnp.where(small < HALF, right, jnp.where(small >= LANES - HALF, left, 0.0))

    def sweeps(l):
        field, push, pull = xe[l], fe[l], be[...]
        for _ in range(HALF):
            near = pltpu.roll(field, 1, 0) + pltpu.roll(field, tall - 1, 0)
            near = near + pltpu.roll(field, 1, 1) + pltpu.roll(field, 2 * LANES - 1, 1)
            field = (1.0 - OMEGA) * field + push + pull * near
        return field[EDGE : EDGE + rows, 0:LANES]

    planes = [functools.partial(lambda l: x_ref[0, l], l) for l in range(levels)]
    planes += [
        functools.partial(lambda l: fe[l, EDGE : EDGE + rows, 0:LANES], l)
        for l in range(levels)
    ]
    planes += [lambda: be[EDGE : EDGE + rows, 0:LANES]]
    pack(planes, rs1, ps1)
    for ref in (rr1, pr1, rr2, pr2):
        ref[...] = jnp.zeros_like(ref)

    barrier = pltpu.get_barrier_semaphore()

    def hello(*device):
        pl.semaphore_signal(barrier, inc=1, device_id=device, device_id_type=MESH)

    total = n_gx + n_gy - 1
    for k in range(1, n_gy):
        hello(sec, gx, lax.rem(gy + k, n_gy))
    for k in range(n_gx):
        hello(1 - sec, lax.rem(gx + k, n_gx), gy)
    for a, b in around:
        if a != 0:
            there = exists(a, b)
            total = total + jnp.where(there, 1, 0)

            @pl.when(there)
            def _():
                hello(sec, gx + a, gy + b)

    pl.semaphore_wait(barrier, total)

    halo_start(0, rs1, rr1, ps1, pr1)

    def table_z(to, slot):
        return pltpu.make_async_remote_copy(
            src_ref=tz.at[gy], dst_ref=tz.at[slot],
            send_sem=tz_send.at[to], recv_sem=tz_recv.at[slot],
            device_id=(sec, gx, to), device_id_type=MESH,
        )

    def table_p(to, slot):
        return pltpu.make_async_remote_copy(
            src_ref=tz.at[gy], dst_ref=tp.at[slot],
            send_sem=tp_send.at[to], recv_sem=tp_recv.at[slot],
            device_id=(1 - sec, to, gy), device_id_type=MESH,
        )

    def others(act):
        def one(k, _):
            act(lax.rem(gy + k, n_gy))
            return 0
        lax.fori_loop(1, n_gy, one, 0)

    def plane(act):
        def one(k, _):
            act(lax.rem(gx + k, n_gx))
            return 0
        lax.fori_loop(0, n_gx, one, 0)

    others(lambda to: table_z(to, gy).start())
    plane(lambda to: table_p(to, gx).start())

    halo_wait(0, rs1, rr1, ps1, pr1)
    for l in range(levels):
        for ref, k in ((xe, l), (fe, levels + l)):
            ref[l, 0:EDGE, 0:LANES] = rr1[0, k]
            ref[l, EDGE + rows : tall, 0:LANES] = rr1[1, k]
            ref[l, :, LANES : 2 * LANES] = beside(pr1, k)
        xe[l, EDGE : EDGE + rows, 0:LANES] = x_ref[0, l]
    be[0:EDGE, 0:LANES] = rr1[0, 2 * levels]
    be[EDGE + rows : tall, 0:LANES] = rr1[1, 2 * levels]
    be[:, LANES : 2 * LANES] = beside(pr1, 2 * levels)

    def z_copy(c, to, slot):
        return pltpu.make_async_remote_copy(
            src_ref=gz.at[gy, pl.ds(c * chunk, chunk)],
            dst_ref=gz.at[slot, pl.ds(c * chunk, chunk)],
            send_sem=z_send.at[c, to], recv_sem=z_recv.at[c, slot],
            device_id=(sec, gx, to), device_id_type=MESH,
        )

    def first(c, _):
        def one(k, _):
            gz[gy, c * chunk + k] = sweeps(c * chunk + k)
            return 0
        lax.fori_loop(0, chunk, one, 0)
        others(lambda to: z_copy(c, to, gy).start())
        return 0

    lax.fori_loop(0, chunks, first, 0)

    others(lambda at: table_z(at, at).wait_recv())
    plane(lambda at: table_p(at, at).wait_recv())
    patch_row = (row // 2).astype(F32)
    same = (row % 2) == (lane % 2)

    def hot(values):
        return jnp.where(values == patch_row, 1.0, 0.0).astype(BF16)

    def counts(a, b, scale):
        both = lax.dot_general(a, b, (((1,), (1,)), ((), ())), preferred_element_type=F32)
        return jnp.where(same, scale * both, 0.0).astype(BF16)

    def build(d, _):
        dest = d * n_gy + gy
        for z in range(n_gy):
            giver = gx * n_gy + z
            given = hot(tz[z, pl.ds(dest, 1), :] - 1.0)
            taken = hot(tz[z, pl.ds(groups + dest, 1), :])
            asked = hot(tp[d, pl.ds(giver, 1), :] - 1.0)
            put = hot(tp[d, pl.ds(groups + giver, 1), :])
            weights[d, 0:LANES, z * LANES : (z + 1) * LANES] = counts(put, given, KAPPA)
            weights[d, LANES : 2 * LANES, z * LANES : (z + 1) * LANES] = counts(
                asked, taken, 1.0
            )
        return 0

    lax.fori_loop(0, n_gx, build, 0)

    def p_copy(c, to, slot):
        return pltpu.make_async_remote_copy(
            src_ref=parts.at[lax.rem(c, 2), to], dst_ref=arrived.at[c, slot],
            send_sem=p_send.at[lax.rem(c, 2), to], recv_sem=p_recv.at[c, slot],
            device_id=(1 - sec, to, gy), device_id_type=MESH,
        )

    def second(c, _):
        others(lambda at: z_copy(c, at, at).wait_recv())
        for z in range(n_gy):
            for k in range(chunk):
                rest = gz[z, c * chunk + k]
                for piece in range(3):
                    cut = rest.astype(BF16)
                    pieces[piece, z * LANES : (z + 1) * LANES, k * LANES : (k + 1) * LANES] = cut
                    rest = rest - cut.astype(F32)

        def one(d):
            @pl.when(c >= 2)
            def _():
                p_copy(c, d, gx).wait_send()

            made = jnp.dot(weights[d], pieces[0], preferred_element_type=F32)
            made = made + jnp.dot(weights[d], pieces[1], preferred_element_type=F32)
            made = made + jnp.dot(weights[d], pieces[2], preferred_element_type=F32)
            for k in range(chunk):
                for h in range(2):
                    parts[lax.rem(c, 2), d, k, h] = made[
                        h * LANES : (h + 1) * LANES, k * LANES : (k + 1) * LANES
                    ]
            p_copy(c, d, gx).start()

        plane(one)
        return 0

    lax.fori_loop(0, chunks, second, 0)

    def third(c, _):
        plane(lambda at: p_copy(c, at, at).wait_recv())

        def one(k, _):
            def add(d, sums):
                return sums[0] + arrived[c, d, k, 0], sums[1] + arrived[c, d, k, 1]

            plain, scaled = lax.fori_loop(
                1, n_gx, add, (arrived[c, 0, k, 0], arrived[c, 0, k, 1])
            )
            old = gz[gy, c * chunk + k]
            xe[c * chunk + k, EDGE : EDGE + rows, 0:LANES] = (
                old + plain + jnp.tanh(old) * scaled
            )
            return 0

        lax.fori_loop(0, chunk, one, 0)
        return 0

    lax.fori_loop(0, chunks, third, 0)

    planes = [
        functools.partial(lambda l: xe[l, EDGE : EDGE + rows, 0:LANES], l)
        for l in range(levels)
    ]
    pack(planes, rs2, ps2)
    halo_start(1, rs2, rr2, ps2, pr2)
    halo_wait(1, rs2, rr2, ps2, pr2)
    for l in range(levels):
        xe[l, 0:EDGE, 0:LANES] = rr2[0, l]
        xe[l, EDGE + rows : tall, 0:LANES] = rr2[1, l]
        xe[l, :, LANES : 2 * LANES] = beside(pr2, l)

    def last(l, _):
        out_ref[0, l] = sweeps(l)
        return 0

    lax.fori_loop(0, levels, last, 0)

    others(lambda to: table_z(to, gy).wait_send())
    plane(lambda to: table_p(to, gx).wait_send())

    def drain(c, _):
        others(lambda to: z_copy(c, to, gy).wait_send())
        return 0

    lax.fori_loop(0, chunks, drain, 0)
    for c in range(max(0, chunks - 2), chunks):
        plane(lambda to: p_copy(c, to, gx).wait_send())


def body(n_gx, n_gy, adjoint_state, forcing, viscosity, reaction, source_patch, owner, cavity_map):
    levels, rows = adjoint_state.shape[1:3]
    groups, cap = cavity_map.shape[2:]
    chunk = 2 if levels % 2 == 0 else 1
    chunks = levels // chunk
    tall = rows + 2 * EDGE
    n1, n2 = 2 * levels + 1, levels
    k1, k2 = -(-n1 // 16), -(-n2 // 16)
    dma = pltpu.SemaphoreType.DMA
    vmem = pl.BlockSpec(memory_space=pltpu.VMEM)
    return pl.pallas_call(
        functools.partial(kernel, n_gx, n_gy, groups, cap, levels, chunk),
        out_shape=jax.ShapeDtypeStruct(adjoint_state.shape, F32),
        in_specs=[vmem] * 7,
        out_specs=vmem,
        scratch_shapes=[
            pltpu.VMEM((levels, tall, 2 * LANES), F32),
            pltpu.VMEM((levels, tall, 2 * LANES), F32),
            pltpu.VMEM((tall, 2 * LANES), F32),
            pltpu.VMEM((2, n1, EDGE, LANES), F32),
            pltpu.VMEM((2, n1, EDGE, LANES), F32),
            pltpu.VMEM((k1, rows, LANES), F32),
            pltpu.VMEM((2, k1, tall, LANES), F32),
            pltpu.VMEM((2, n2, EDGE, LANES), F32),
            pltpu.VMEM((2, n2, EDGE, LANES), F32),
            pltpu.VMEM((k2, rows, LANES), F32),
            pltpu.VMEM((2, k2, tall, LANES), F32),
            pltpu.VMEM((n_gy, 2 * groups, LANES), F32),
            pltpu.VMEM((n_gx, 2 * groups, LANES), F32),
            pltpu.VMEM((n_gx, 2 * LANES, n_gy * LANES), BF16),
            pltpu.VMEM((3, n_gy * LANES, chunk * LANES), BF16),
            pltpu.VMEM((n_gy, levels, rows, LANES), F32),
            pltpu.VMEM((2, n_gx, chunk, 2, rows, LANES), F32),
            pltpu.VMEM((chunks, n_gx, chunk, 2, rows, LANES), F32),
            dma((2, 8)), dma((2, 8)),
            dma((n_gy,)), dma((n_gy,)), dma((n_gx,)), dma((n_gx,)),
            dma((chunks, n_gy)), dma((chunks, n_gy)), dma((2, n_gx)), dma((chunks, n_gx)),
        ],
        compiler_params=pltpu.CompilerParams(
            collective_id=0, has_side_effects=True, vmem_limit_bytes=60 * 2**20
        ),
    )(adjoint_state, forcing, viscosity, reaction, source_patch, owner, cavity_map)


def solution(mesh):
    return jax.shard_map(
        functools.partial(body, mesh.shape["gx"], mesh.shape["gy"]),
        mesh=mesh,
        in_specs=(
            P("sec", None, "gx", "gy"),
            P("sec", None, "gx", "gy"),
            P("sec", "gx", "gy"),
            P("sec", "gx", "gy"),
            P("sec", ("gx", "gy")),
            P("sec", ("gx", "gy"), None),
            P("sec", ("gx", "gy"), None, None),
        ),
        out_specs=P("sec", None, "gx", "gy"),
        check_vma=False,
    )
```

time: 378 us -> 114 us (0.30); the launches traced: 374 us -> 114 us
  Pallas kernels: 0 us -> 111 us
  waiting for transfers between devices: 105 us -> 0 us
  starting transfers between devices: 91.7 us -> 0 us
  blocking collectives: 64 us -> 0 us
  other arithmetic: 62 us -> 0 us
  local copies, waits for them, and re-layouts: 50.3 us -> 3.36 us
    pallas_call x0 -> x1, Pallas kernels: none -> 111 us  [body(): pl.pallas_call(functools.partial(kernel, n_gx, n_gy, groups, cap, levels,...]
    ppermute x34 -> x0, starting transfers between devices: 84.8 us -> none  [the longest x16 63.8 us: extended(): lax.ppermute(tail, axis, [(i, (i + 1) % count) for i in range(ends)])]
    all_to_all x1 -> x0, blocking collectives: 64 us -> none  [couple(): lax.all_to_all(answer, ('gx', 'gy'), split_axis=0, concat_axis=0, tiled=T...]
    all_to_all x1 -> x0, waiting for transfers between devices: 57.8 us -> none  [couple(): lax.all_to_all(crossed, ('gx', 'gy'), split_axis=0, concat_axis=0, tiled=...]
    ppermute x34 -> x0, waiting for transfers between devices: 47.2 us -> none  [the longest x16 31.8 us: extended(): lax.ppermute(head, axis, [((i + 1) % count, i) for i in range(ends)])]
    scatter-add x2 -> x0, other arithmetic: 42.6 us -> none  [the longest x1 31 us: couple(): updated = grid.at[:, tgt_band, :, tgt_strip, :].add(KAPPA * arrived)]
    scatter x1 -> x0, local copies, waits for them, and re-layouts: 15.5 us -> none  [couple(): jnp.zeros((groups * slots_per, levels, PATCH, PW), jnp.float32).at[slot]]
    gather x3 -> x0, local copies, waits for them, and re-layouts: 13.1 us -> none  [the longest x1 5.85 us: couple(): local = grid[:, tgt_band, :, tgt_strip, :]]
  transfers between devices with their start and end apart: 35 -> 0, of which waited for: 18 -> 0; matrix products, arithmetic and copies ran while one was open for 12% -> 0% of each run, Pallas kernels for 0% -> 0%
where the time goes in v1:
time: 114 us
  Pallas kernels  111 us (97%)
  local copies, waits for them, and re-layouts  3.36 us (3%)
    pallas_call x1, Pallas kernels, body(): pl.pallas_call(functools.partial(kernel, n_gx, n_gy, groups, cap, levels,...  111 us
    unnamed x2, local copies, waits for them, and re-layouts  3.36 us

profile of v1, /device:TPU:0, one launch (start us, length us, event | category | flops | bytes accessed | tf_op | source)
XLA Modules:
  0.0 114.0 jit_solution(6742681732214088108)
XLA Ops:
  0.0 1.4 %copy.8.own_ref = s32[1,128,1]{2,1,0:T(8,128)} copy(s32[1,128,1]{1,2,0:T(1,128)} %param.12) | data formatting | bytes 1024 | tf_op args[5]
  1.4 110.7 %shard_map.73 = f32[1,10,128,128]{3,2,1,0:T(8,128)} custom-call(f32[1,10,128,128]{3,2,1,0:T(8,128)} %x_ref.1, f32[1,10,128,128]{3,2,1,0:T(8,128)} %f_ref.1, f32[1,128,128]{2,1,0:T(8,128)} %v_ref.1, f32[1,128,128]{2,1,0:T(8,128)} %r_ref.1, s32[1,128]{1,0:T(1,128)} %src_ref.1, s32[1,128,1]{2,1,0:T(8,128)} %copy.8.own_ref, s32[1,1,16,16]{3,2,1,0:T(8,128)} %map_ref.1), custom_call_target="tpu_custom_call" | custom-call | tf_op jit(solution)/shard_map/pallas_call | solution.py:351
  112.1 2.0 %copy.10 = f32[1,10,128,128]{3,2,1,0:T(8,128)} copy(f32[1,10,128,128]{3,2,1,0:T(8,128)} %shard_map.73) | data formatting | bytes 1310720

commit v2 on v1

--- a/solution.py
+++ b/solution.py
@@ -22,12 +22,12 @@
 
 
 def kernel(
-    n_gx, n_gy, groups, cap, levels, chunk,
+    n_gx, n_gy, groups, cap, levels, chunk, square,
     x_ref, f_ref, v_ref, r_ref, src_ref, own_ref, map_ref, out_ref,
     xe, fe, be, rs1, rr1, ps1, pr1, rs2, rr2, ps2, pr2,
-    tz, tp, weights, pieces, gz, parts, arrived,
-    halo_send, halo_recv, tz_send, tz_recv, tp_send, tp_recv,
-    z_send, z_recv, p_send, p_recv,
+    tz, tp, weights, pieces, gz, parts, relay, arrived,
+    halo_send, halo_recv, halo_send2, halo_recv2, tz_send, tz_recv, tp_send, tp_recv,
+    z_send, z_recv, p_send, p_recv, r_send, r_recv,
 ):
     sec, gx, gy = lax.axis_index("sec"), lax.axis_index("gx"), lax.axis_index("gy")
     rows = x_ref.shape[2]
@@ -36,6 +36,17 @@
     has = {-1: gx > 0, 0: True, 1: gx < n_gx - 1}
     has_y = {-1: gy > 0, 0: True, 1: gy < n_gy - 1}
     around = [(a, b) for a in (-1, 0, 1) for b in (-1, 0, 1) if (a, b) != (0, 0)]
+
+    def beyond(e):
+        if not square:
+            return lax.rem(gx + e, n_gx)
+        if e == 0:
+            return gx
+        if e == 1:
+            return gx + 1 - 2 * (gx % 2)
+        if e == 2:
+            return gx + 2 - 4 * (gx // 2)
+        return n_gx - 1 - gx
 
     def exists(a, b):
         if a == 0:
@@ -81,7 +92,7 @@
                 packed = jnp.where(small // 4 == 2 * k + 1, high, packed)
             ps[first // 16] = packed
 
-    def halo_copy(phase, a, b, rs, rr, ps, pr):
+    def halo_copy(a, b, rs, rr, ps, pr, ss, sr):
         if b == 0:
             src, dst = rs.at[(a + 1) // 2], rr.at[(1 - a) // 2]
         else:
@@ -95,25 +106,32 @@
         k = around.index((a, b))
         return pltpu.make_async_remote_copy(
             src_ref=src, dst_ref=dst,
-            send_sem=halo_send.at[phase, k], recv_sem=halo_recv.at[phase, k],
+            send_sem=ss.at[k], recv_sem=sr.at[k],
             device_id=(sec, gx + a, gy + b), device_id_type=MESH,
         )
 
-    def halo_start(phase, *refs):
+    def halo_start(refs):
         for a, b in around:
             @pl.when(exists(a, b))
             def _():
-                halo_copy(phase, a, b, *refs).start()
-
-    def halo_wait(phase, rs, rr, ps, pr):
+                halo_copy(a, b, *refs).start()
+
+    def halo_wait(refs):
         for a, b in around:
             @pl.when(exists(-a, -b))
             def _():
-                halo_copy(phase, a, b, rs, rr, ps, pr).wait_recv()
-
+                halo_copy(a, b, *refs).wait_recv()
+
+    def halo_sent(refs):
+        for a, b in around:
             @pl.when(exists(a, b))
             def _():
-                halo_copy(phase, a, b, rs, rr, ps, pr).wait_send()
+                halo_copy(a, b, *refs).wait_send()
+
+    halo1 = (rs1, rr1, ps1, pr1, halo_send, halo_recv)
+
+    def halo2(c):
+        return tuple(r.at[c] for r in (rs2, rr2, ps2, pr2, halo_send2, halo_recv2))
 
     def beside(pr, k):
         small = iota((tall, LANES), 1)
@@ -160,9 +178,13 @@
             def _():
                 hello(sec, gx + a, gy + b)
 
+    if square:
+        total = total + 2
+        for e in (1, 2):
+            hello(sec, beyond(e), gy)
     pl.semaphore_wait(barrier, total)
 
-    halo_start(0, rs1, rr1, ps1, pr1)
+    halo_start(halo1)
 
     def table_z(to, slot):
         return pltpu.make_async_remote_copy(
@@ -193,7 +215,7 @@
     others(lambda to: table_z(to, gy).start())
     plane(lambda to: table_p(to, gx).start())
 
-    halo_wait(0, rs1, rr1, ps1, pr1)
+    halo_wait(halo1)
     for l in range(levels):
         for ref, k in ((xe, l), (fe, levels + l)):
             ref[l, 0:EDGE, 0:LANES] = rr1[0, k]
@@ -204,23 +226,39 @@
     be[EDGE + rows : tall, 0:LANES] = rr1[1, 2 * levels]
     be[:, LANES : 2 * LANES] = beside(pr1, 2 * levels)
 
-    def z_copy(c, to, slot):
-        return pltpu.make_async_remote_copy(
-            src_ref=gz.at[gy, pl.ds(c * chunk, chunk)],
+    def z_copy(step, c, slot):
+        return pltpu.make_async_remote_copy(
+            src_ref=gz.at[slot, pl.ds(c * chunk, chunk)],
             dst_ref=gz.at[slot, pl.ds(c * chunk, chunk)],
-            send_sem=z_send.at[c, to], recv_sem=z_recv.at[c, slot],
-            device_id=(sec, gx, to), device_id_type=MESH,
-        )
-
-    def first(c, _):
+            send_sem=z_send.at[(step + 1) // 2, c, slot], recv_sem=z_recv.at[c, slot],
+            device_id=(sec, gx, gy + step), device_id_type=MESH,
+        )
+
+    def z_start(step, c, slot):
+        @pl.when(has_y[step])
+        def _():
+            z_copy(step, c, slot).start()
+
+    def first(c):
         def one(k, _):
             gz[gy, c * chunk + k] = sweeps(c * chunk + k)
             return 0
         lax.fori_loop(0, chunk, one, 0)
-        others(lambda to: z_copy(c, to, gy).start())
-        return 0
-
-    lax.fori_loop(0, chunks, first, 0)
+        z_start(1, c, gy)
+        z_start(-1, c, gy)
+
+    def onward(c, d):
+        @pl.when(gy >= d)
+        def _():
+            z_copy(1, c, gy - d).wait_recv()
+            z_start(1, c, gy - d)
+
+        @pl.when(gy + d < n_gy)
+        def _():
+            z_copy(-1, c, gy + d).wait_recv()
+            z_start(-1, c, gy + d)
+
+    first(0)
 
     others(lambda at: table_z(at, at).wait_recv())
     plane(lambda at: table_p(at, at).wait_recv())
@@ -250,15 +288,31 @@
 
     lax.fori_loop(0, n_gx, build, 0)
 
-    def p_copy(c, to, slot):
-        return pltpu.make_async_remote_copy(
-            src_ref=parts.at[lax.rem(c, 2), to], dst_ref=arrived.at[c, slot],
-            send_sem=p_send.at[lax.rem(c, 2), to], recv_sem=p_recv.at[c, slot],
-            device_id=(1 - sec, to, gy), device_id_type=MESH,
-        )
-
-    def second(c, _):
-        others(lambda at: z_copy(c, at, at).wait_recv())
+    def part_slot(c):
+        return c if square else lax.rem(c, 2)
+
+    def whole(c, e):
+        return pltpu.make_async_remote_copy(
+            src_ref=parts.at[part_slot(c), e], dst_ref=arrived.at[c, e],
+            send_sem=p_send.at[part_slot(c), e, 0], recv_sem=p_recv.at[c, e, 0],
+            device_id=(1 - sec, beyond(e), gy), device_id_type=MESH,
+        )
+
+    def single(c, e, k):
+        return pltpu.make_async_remote_copy(
+            src_ref=parts.at[c, e, k], dst_ref=arrived.at[c, e, k],
+            send_sem=p_send.at[c, e, k], recv_sem=p_recv.at[c, e, k],
+            device_id=(1 - sec, beyond(e), gy), device_id_type=MESH,
+        )
+
+    def corner(c, k):
+        return pltpu.make_async_remote_copy(
+            src_ref=parts.at[c, 3, k], dst_ref=relay.at[c, k],
+            send_sem=r_send.at[c, k], recv_sem=r_recv.at[c, k],
+            device_id=(sec, beyond(1 + k), gy), device_id_type=MESH,
+        )
+
+    def second(c):
         for z in range(n_gy):
             for k in range(chunk):
                 rest = gz[z, c * chunk + k]
@@ -267,75 +321,133 @@
                     pieces[piece, z * LANES : (z + 1) * LANES, k * LANES : (k + 1) * LANES] = cut
                     rest = rest - cut.astype(F32)
 
-        def one(d):
-            @pl.when(c >= 2)
-            def _():
-                p_copy(c, d, gx).wait_send()
-
-            made = jnp.dot(weights[d], pieces[0], preferred_element_type=F32)
-            made = made + jnp.dot(weights[d], pieces[1], preferred_element_type=F32)
-            made = made + jnp.dot(weights[d], pieces[2], preferred_element_type=F32)
+        def make(e):
+            w = weights[beyond(e)]
+            made = jnp.dot(w, pieces[0], preferred_element_type=F32)
+            made = made + jnp.dot(w, pieces[1], preferred_element_type=F32)
+            made = made + jnp.dot(w, pieces[2], preferred_element_type=F32)
             for k in range(chunk):
                 for h in range(2):
-                    parts[lax.rem(c, 2), d, k, h] = made[
+                    parts[part_slot(c), e, k, h] = made[
                         h * LANES : (h + 1) * LANES, k * LANES : (k + 1) * LANES
                     ]
-            p_copy(c, d, gx).start()
-
-        plane(one)
-        return 0
-
-    lax.fori_loop(0, chunks, second, 0)
-
-    def third(c, _):
-        plane(lambda at: p_copy(c, at, at).wait_recv())
-
-        def one(k, _):
-            def add(d, sums):
-                return sums[0] + arrived[c, d, k, 0], sums[1] + arrived[c, d, k, 1]
+
+        if square:
+            make(3)
+            corner(c, 0).start()
+            corner(c, 1).start()
+            make(1)
+            single(c, 1, 0).start()
+            make(2)
+            single(c, 2, 1).start()
+            make(0)
+            whole(c, 0).start()
+        else:
+            def one(e, _):
+                @pl.when(c >= 2)
+                def _():
+                    whole(c, e).wait_send()
+                make(e)
+                whole(c, e).start()
+                return 0
+            lax.fori_loop(0, n_gx, one, 0)
+
+    def combine(c):
+        if square:
+            for k in range(2):
+                corner(c, k).wait_recv()
+                for h in range(2):
+                    parts[c, 2 - k, k, h] = parts[c, 2 - k, k, h] + relay[c, k, h]
+                single(c, 2 - k, k).start()
+
+    def third(c):
+        if square:
+            whole(c, 0).wait_recv()
+            for e in (1, 2):
+                for k in range(2):
+                    single(c, e, k).wait_recv()
+        else:
+            def arrive(e, _):
+                whole(c, e).wait_recv()
+                return 0
+            lax.fori_loop(0, n_gx, arrive, 0)
+        count = 3 if square else n_gx
+        planes = []
+        for k in range(chunk):
+            def add(e, sums):
+                return sums[0] + arrived[c, e, k, 0], sums[1] + arrived[c, e, k, 1]
 
             plain, scaled = lax.fori_loop(
-                1, n_gx, add, (arrived[c, 0, k, 0], arrived[c, 0, k, 1])
+                1, count, add, (arrived[c, 0, k, 0], arrived[c, 0, k, 1])
             )
             old = gz[gy, c * chunk + k]
-            xe[c * chunk + k, EDGE : EDGE + rows, 0:LANES] = (
-                old + plain + jnp.tanh(old) * scaled
-            )
+            new = old + plain + jnp.tanh(old) * scaled
+            xe[c * chunk + k, EDGE : EDGE + rows, 0:LANES] = new
+            planes.append(functools.partial(lambda new: new, new))
+        pack(planes, rs2.at[c], ps2.at[c])
+        halo_start(halo2(c))
+
+    def last(c):
+        halo_wait(halo2(c))
+        for k in range(chunk):
+            l = c * chunk + k
+            xe[l, 0:EDGE, 0:LANES] = rr2[c, 0, k]
+            xe[l, EDGE + rows : tall, 0:LANES] = rr2[c, 1, k]
+            xe[l, :, LANES : 2 * LANES] = beside(pr2.at[c], k)
+
+        def one(k, _):
+            out_ref[0, c * chunk + k] = sweeps(c * chunk + k)
             return 0
-
         lax.fori_loop(0, chunk, one, 0)
+
+    stages = [first] + [functools.partial(lambda d, c: onward(c, d), d) for d in range(1, n_gy)]
+    lags = list(range(n_gy)) + [n_gy - 1, n_gy, n_gy + 1, n_gy + 2]
+    stages += [second, combine, third, last]
+
+    def turn(i, _):
+        for lag, stage in zip(lags, stages):
+            c = i - lag
+
+            @pl.when(jnp.logical_and(c >= (1 if lag == 0 else 0), c < chunks))
+            def _():
+                stage(c)
         return 0
 
-    lax.fori_loop(0, chunks, third, 0)
-
-    planes = [
-        functools.partial(lambda l: xe[l, EDGE : EDGE + rows, 0:LANES], l)
-        for l in range(levels)
-    ]
-    pack(planes, rs2, ps2)
-    halo_start(1, rs2, rr2, ps2, pr2)
-    halo_wait(1, rs2, rr2, ps2, pr2)
-    for l in range(levels):
-        xe[l, 0:EDGE, 0:LANES] = rr2[0, l]
-        xe[l, EDGE + rows : tall, 0:LANES] = rr2[1, l]
-        xe[l, :, LANES : 2 * LANES] = beside(pr2, l)
-
-    def last(l, _):
-        out_ref[0, l] = sweeps(l)
-        return 0
-
-    lax.fori_loop(0, levels, last, 0)
+    lax.fori_loop(1, chunks + lags[-1], turn, 0)
 
     others(lambda to: table_z(to, gy).wait_send())
     plane(lambda to: table_p(to, gx).wait_send())
+    halo_sent(halo1)
 
     def drain(c, _):
-        others(lambda to: z_copy(c, to, gy).wait_send())
+        halo_sent(halo2(c))
+
+        def slot(z, _):
+            @pl.when(jnp.logical_and(z <= gy, has_y[1]))
+            def _():
+                z_copy(1, c, z).wait_send()
+
+            @pl.when(jnp.logical_and(z >= gy, has_y[-1]))
+            def _():
+                z_copy(-1, c, z).wait_send()
+            return 0
+
+        lax.fori_loop(0, n_gy, slot, 0)
+        if square:
+            whole(c, 0).wait_send()
+            for k in range(2):
+                corner(c, k).wait_send()
+                for e in (1, 2):
+                    single(c, e, k).wait_send()
         return 0
 
     lax.fori_loop(0, chunks, drain, 0)
-    for c in range(max(0, chunks - 2), chunks):
-        plane(lambda to: p_copy(c, to, gx).wait_send())
+    if not square:
+        for c in range(max(0, chunks - 2), chunks):
+            def left(e, _):
+                whole(c, e).wait_send()
+                return 0
+            lax.fori_loop(0, n_gx, left, 0)
 
 
 def body(n_gx, n_gy, adjoint_state, forcing, viscosity, reaction, source_patch, owner, cavity_map):
@@ -344,12 +456,15 @@
     chunk = 2 if levels % 2 == 0 else 1
     chunks = levels // chunk
     tall = rows + 2 * EDGE
-    n1, n2 = 2 * levels + 1, levels
-    k1, k2 = -(-n1 // 16), -(-n2 // 16)
+    n1 = 2 * levels + 1
+    k1 = -(-n1 // 16)
+    square = n_gx == 4 and chunk == 2
+    slots = chunks if square else 2
+    roles = 3 if square else n_gx
     dma = pltpu.SemaphoreType.DMA
     vmem = pl.BlockSpec(memory_space=pltpu.VMEM)
     return pl.pallas_call(
-        functools.partial(kernel, n_gx, n_gy, groups, cap, levels, chunk),
+        functools.partial(kernel, n_gx, n_gy, groups, cap, levels, chunk, square),
         out_shape=jax.ShapeDtypeStruct(adjoint_state.shape, F32),
         in_specs=[vmem] * 7,
         out_specs=vmem,
@@ -361,20 +476,23 @@
             pltpu.VMEM((2, n1, EDGE, LANES), F32),
             pltpu.VMEM((k1, rows, LANES), F32),
             pltpu.VMEM((2, k1, tall, LANES), F32),
-            pltpu.VMEM((2, n2, EDGE, LANES), F32),
-            pltpu.VMEM((2, n2, EDGE, LANES), F32),
-            pltpu.VMEM((k2, rows, LANES), F32),
-            pltpu.VMEM((2, k2, tall, LANES), F32),
+            pltpu.VMEM((chunks, 2, chunk, EDGE, LANES), F32),
+            pltpu.VMEM((chunks, 2, chunk, EDGE, LANES), F32),
+            pltpu.VMEM((chunks, 1, rows, LANES), F32),
+            pltpu.VMEM((chunks, 2, 1, tall, LANES), F32),
             pltpu.VMEM((n_gy, 2 * groups, LANES), F32),
             pltpu.VMEM((n_gx, 2 * groups, LANES), F32),
             pltpu.VMEM((n_gx, 2 * LANES, n_gy * LANES), BF16),
             pltpu.VMEM((3, n_gy * LANES, chunk * LANES), BF16),
             pltpu.VMEM((n_gy, levels, rows, LANES), F32),
-            pltpu.VMEM((2, n_gx, chunk, 2, rows, LANES), F32),
-            pltpu.VMEM((chunks, n_gx, chunk, 2, rows, LANES), F32),
-            dma((2, 8)), dma((2, 8)),
+            pltpu.VMEM((slots, n_gx, chunk, 2, rows, LANES), F32),
+            pltpu.VMEM((chunks, 2, 2, rows, LANES) if square else (8, LANES), F32),
+            pltpu.VMEM((chunks, roles, chunk, 2, rows, LANES), F32),
+            dma((8,)), dma((8,)), dma((chunks, 8)), dma((chunks, 8)),
             dma((n_gy,)), dma((n_gy,)), dma((n_gx,)), dma((n_gx,)),
-            dma((chunks, n_gy)), dma((chunks, n_gy)), dma((2, n_gx)), dma((chunks, n_gx)),
+            dma((2, chunks, n_gy)), dma((chunks, n_gy)),
+            dma((slots, n_gx, chunk)), dma((chunks, roles, chunk)),
+            dma((chunks, 2)), dma((chunks, 2)),
         ],
         compiler_params=pltpu.CompilerParams(
             collective_id=0, has_side_effects=True, vmem_limit_bytes=60 * 2**20

time: 114 us -> 93.4 us (0.82)
  Pallas kernels: 111 us -> 89.9 us
    pallas_call x1, Pallas kernels: 111 us -> 89.9 us  [body(): pl.pallas_call(functools.partial(kernel, n_gx, n_gy, groups, cap, levels,...]
where the time goes in v2:
time: 93.4 us; the launch traced here: 93.2 us
  Pallas kernels  89.9 us (96%)
  local copies, waits for them, and re-layouts  3.36 us (4%)
    pallas_call x1, Pallas kernels, body(): pl.pallas_call(functools.partial(kernel, n_gx, n_gy, groups, cap, levels,...  89.9 us
    unnamed x2, local copies, waits for them, and re-layouts  3.36 us

profile of v2, /device:TPU:0, one launch (start us, length us, event | category | flops | bytes accessed | tf_op | source)
XLA Modules:
  0.0 93.2 jit_solution(6044841737229834972)
XLA Ops:
  0.0 1.4 %copy.8.own_ref = s32[1,128,1]{2,1,0:T(8,128)} copy(s32[1,128,1]{1,2,0:T(1,128)} %param.12) | data formatting | bytes 1024 | tf_op args[5]
  1.4 89.9 %shard_map.73 = f32[1,10,128,128]{3,2,1,0:T(8,128)} custom-call(f32[1,10,128,128]{3,2,1,0:T(8,128)} %x_ref.1, f32[1,10,128,128]{3,2,1,0:T(8,128)} %f_ref.1, f32[1,128,128]{2,1,0:T(8,128)} %v_ref.1, f32[1,128,128]{2,1,0:T(8,128)} %r_ref.1, s32[1,128]{1,0:T(1,128)} %src_ref.1, s32[1,128,1]{2,1,0:T(8,128)} %copy.8.own_ref, s32[1,1,16,16]{3,2,1,0:T(8,128)} %map_ref.1), custom_call_target="tpu_custom_call" | custom-call | tf_op jit(solution)/shard_map/pallas_call | solution.py:466
  91.3 2.0 %copy.10 = f32[1,10,128,128]{3,2,1,0:T(8,128)} copy(f32[1,10,128,128]{3,2,1,0:T(8,128)} %shard_map.73) | data formatting | bytes 1310720

commit v3 on v2

--- a/solution.py
+++ b/solution.py
@@ -57,7 +57,10 @@
 
     lane = iota((LANES, LANES), 1)
     row = iota((LANES, LANES), 0)
-    named = jnp.where(own_ref[0] == lane, 1.0, 0.0).astype(BF16)
+    owner = jnp.sum(
+        jnp.where(lane == row, own_ref[...].astype(F32), 0.0), axis=1, keepdims=True
+    )
+    named = jnp.where(owner == lane.astype(F32), 1.0, 0.0).astype(BF16)
     earlier = jnp.where(lane < row, 1.0, 0.0).astype(BF16)
     before = jnp.dot(earlier, named, preferred_element_type=F32)
     rank = jnp.sum(before * named.astype(F32), axis=1, keepdims=True)
@@ -497,7 +500,7 @@
         compiler_params=pltpu.CompilerParams(
             collective_id=0, has_side_effects=True, vmem_limit_bytes=60 * 2**20
         ),
-    )(adjoint_state, forcing, viscosity, reaction, source_patch, owner, cavity_map)
+    )(adjoint_state, forcing, viscosity, reaction, source_patch, owner[:, :, 0], cavity_map)
 
 
 def solution(mesh):

time: 93.4 us -> 92 us (0.985)
  local copies, waits for them, and re-layouts: 3.36 us -> 1.97 us
    unnamed x2 -> x1, local copies, waits for them, and re-layouts: 3.36 us -> 1.97 us
where the time goes in v3:
time: 92 us; the launch traced here: 91.8 us
  Pallas kernels  89.8 us (98%)
  local copies, waits for them, and re-layouts  1.97 us (2%)
    pallas_call x1, Pallas kernels, body(): pl.pallas_call(functools.partial(kernel, n_gx, n_gy, groups, cap, levels,...  89.8 us
    unnamed x1, local copies, waits for them, and re-layouts  1.97 us

profile of v3, /device:TPU:0, one launch (start us, length us, event | category | flops | bytes accessed | tf_op | source)
XLA Modules:
  0.0 91.8 jit_solution(15326355896796501547)
XLA Ops:
  0.0 89.8 %shard_map.73 = f32[1,10,128,128]{3,2,1,0:T(8,128)} custom-call(f32[1,10,128,128]{3,2,1,0:T(8,128)} %x_ref.1, f32[1,10,128,128]{3,2,1,0:T(8,128)} %f_ref.1, f32[1,128,128]{2,1,0:T(8,128)} %v_ref.1, f32[1,128,128]{2,1,0:T(8,128)} %r_ref.1, s32[1,128]{1,0:T(1,128)} %src_ref.1, s32[1,128]{1,0:T(1,128)} %bitcast.1, s32[1,1,16,16]{3,2,1,0:T(8,128)} %map_ref.1), custom_call_target="tpu_custom_call" | custom-call | tf_op jit(solution)/shard_map/pallas_call | solution.py:469
  89.8 2.0 %copy.9 = f32[1,10,128,128]{3,2,1,0:T(8,128)} copy(f32[1,10,128,128]{3,2,1,0:T(8,128)} %shard_map.73) | data formatting | bytes 1310720
